TPU v7x, 512 devices: a whole 4x4x16 slice. The times are simulated.
512 devices in a mesh: blk: 128 (over x, z, y_hi), grp: 4 (over y_lo, core).
Axes of the slice: x: 4, y: 4 (y_hi: 2, y_lo: 2; y = y_hi * 2 + y_lo), z: 16, core: 2. Of those that a mesh axis runs over, the one named last changes fastest.
Arguments:
- molecules: bfloat16 [16384, 640], P(('blk', 'grp')), may hold values from -2 to 2
- texts: bfloat16 [16384, 640], P(('blk', 'grp')), may hold values from -2 to 2
Outputs:
- molecule_grad: float32 [16384, 640], P(('blk', 'grp'))
- text_grad: float32 [16384, 640], P(('blk', 'grp'))
All inputs are finite; a program needn't handle non-finite values.
Results may differ from a plain program's by a relative error of at most 0.0055.
Values may be sent and summed in bfloat16 or wider, within the bound.
A program may use at most 64 MiB of HBM per device.

v0:
```python
import jax
import jax.numpy as jnp
from jax import lax
from jax.sharding import PartitionSpec as P

INVERSE_TEMP = 1.0 / 0.07
NEG_FILL = -1e30


def merged(x, axis, combine):
    everything = jax.tree.map(lambda part: lax.all_gather(part, axis), x)
    first = jax.tree.map(lambda part: part[0], everything)

    def step(k, so_far):
        return combine(so_far, jax.tree.map(lambda part: part[k], everything))

    return lax.fori_loop(1, lax.axis_size(axis), step, first)


def piece_size(length):
    return max((divisor for divisor in range(1, min(length, 512) + 1) if length % divisor == 0))


def split_blocks(array, size):
    return array.reshape((array.shape[0] // size, size) + array.shape[1:])


def merge_pair(first_pair, second_pair):
    raised = jnp.maximum(first_pair[0], second_pair[0])
    return (
        raised,
        first_pair[1] * jnp.exp(first_pair[0] - raised)
        + second_pair[1] * jnp.exp(second_pair[0] - raised),
    )


def run_sides(anchor, other):
    shard_rows, features = anchor.shape
    group_size = lax.axis_size("grp")
    cycle_size = lax.axis_size("blk")
    block_index = lax.axis_index("blk")
    group_index = lax.axis_index("grp")
    anchor_block = lax.all_gather(anchor, "grp", axis=0, tiled=True)
    height = anchor_block.shape[0]
    column_count = shard_rows * cycle_size
    row_ids = block_index * height + jnp.arange(height, dtype=jnp.int32)

    def global_ids(positions):
        return (
            positions // shard_rows * group_size + group_index
        ) * shard_rows + positions % shard_rows

    initial = (
        jnp.full((height,), NEG_FILL, jnp.float32),
        jnp.zeros((height,), jnp.float32),
        jnp.zeros((column_count,), jnp.float32),
        jnp.zeros((column_count,), jnp.float32),
    )
    segment = lax.all_gather(other, "blk", axis=0, tiled=True)
    first_row = jnp.int32(0)
    size = piece_size(segment.shape[0])

    def stats_advance(running, element):
        other_block, offset = element
        row_top, row_mass, column_top, column_mass = running
        scores = (
            jnp.einsum("ad,kd->ak", anchor_block, other_block, preferred_element_type=jnp.float32)
            * INVERSE_TEMP
        )
        raised = jnp.maximum(row_top, jnp.max(scores, axis=1))
        row_mass = row_mass * jnp.exp(row_top - raised) + jnp.sum(
            jnp.exp(scores - raised[:, None]), axis=1
        )
        local_top = jnp.max(scores, axis=0)
        local_mass = jnp.sum(jnp.exp(scores - local_top[None, :]), axis=0)
        column_top = lax.dynamic_update_slice_in_dim(column_top, local_top, first_row + offset, 0)
        column_mass = lax.dynamic_update_slice_in_dim(
            column_mass, local_mass, first_row + offset, 0
        )
        return ((raised, row_mass, column_top, column_mass), None)

    offsets = jnp.arange(segment.shape[0] // size, dtype=jnp.int32) * size
    running, _ = lax.scan(stats_advance, initial, (split_blocks(segment, size), offsets))
    row_top, row_mass, column_top, column_mass = running
    overall_top = lax.pmax(column_top, "blk")
    column_mass = lax.psum(column_mass * jnp.exp(column_top - overall_top), "blk")
    column_top = overall_top
    col_lse = column_top + jnp.log(column_mass)
    row_top, row_mass = merged((row_top, row_mass), "grp", merge_pair)
    row_lse = row_top + jnp.log(row_mass)
    segment = lax.all_gather(other, "blk", axis=0, tiled=True)
    grad_first_row = jnp.int32(0)
    size = piece_size(segment.shape[0])

    def grad_advance(running, element):
        other_block, offset = element
        positions = grad_first_row + offset + jnp.arange(size, dtype=jnp.int32)
        scores = (
            jnp.einsum("ad,kd->ak", anchor_block, other_block, preferred_element_type=jnp.float32)
            * INVERSE_TEMP
        )
        lse_slice = lax.dynamic_slice_in_dim(col_lse, grad_first_row + offset, size)
        paired = (row_ids[:, None] == global_ids(positions)[None, :]).astype(jnp.float32)
        weights = (
            0.5 * jnp.exp(scores - row_lse[:, None])
            + 0.5 * jnp.exp(scores - lse_slice[None, :])
            - paired
        ).astype(jnp.bfloat16)
        return (
            running
            + jnp.dot(weights, other_block, preferred_element_type=jnp.float32) * INVERSE_TEMP,
            None,
        )

    offsets = jnp.arange(segment.shape[0] // size, dtype=jnp.int32) * size
    running, _ = lax.scan(
        grad_advance,
        jnp.zeros((height, features), jnp.float32),
        (split_blocks(segment, size), offsets),
    )
    partial_anchor = running
    anchor_grad = lax.psum_scatter(partial_anchor, "grp", scatter_dimension=0, tiled=True)
    fixed_block = lax.all_gather(other, "grp", axis=0, tiled=True)
    own_rows = lax.dynamic_slice_in_dim(row_lse, group_index * shard_rows, shard_rows)
    every_lse = lax.all_gather(own_rows, "blk", axis=0, tiled=True)
    own_columns = lax.dynamic_slice_in_dim(col_lse, block_index * shard_rows, shard_rows)
    fixed_lse = lax.all_gather(own_columns, "grp", axis=0, tiled=True)
    segment = lax.all_gather(anchor, "blk", axis=0, tiled=True)
    other_first_row = jnp.int32(0)
    other_size = piece_size(segment.shape[0])

    def other_advance(running, element):
        moving_block, offset = element
        positions = other_first_row + offset + jnp.arange(other_size, dtype=jnp.int32)
        lse_slice = lax.dynamic_slice_in_dim(every_lse, other_first_row + offset, other_size)
        scores = (
            jnp.einsum("kd,rd->kr", moving_block, fixed_block, preferred_element_type=jnp.float32)
            * INVERSE_TEMP
        )
        paired = (global_ids(positions)[:, None] == row_ids[None, :]).astype(jnp.float32)
        weights = (
            0.5 * jnp.exp(scores - lse_slice[:, None])
            + 0.5 * jnp.exp(scores - fixed_lse[None, :])
            - paired
        ).astype(jnp.bfloat16)
        return (
            running
            + jnp.einsum("kr,kd->rd", weights, moving_block, preferred_element_type=jnp.float32)
            * INVERSE_TEMP,
            None,
        )

    offsets = jnp.arange(segment.shape[0] // other_size, dtype=jnp.int32) * other_size
    running, _ = lax.scan(
        other_advance,
        jnp.zeros((height, features), jnp.float32),
        (split_blocks(segment, other_size), offsets),
    )
    other_grad = lax.psum_scatter(running, "grp", scatter_dimension=0, tiled=True)
    return (anchor_grad, other_grad)


def on_device(molecules, texts):
    molecule_grad, text_grad = run_sides(molecules, texts)
    return (molecule_grad, text_grad)


def solution(mesh):
    in_specs = (P(("blk", "grp"), None), P(("blk", "grp"), None))
    out_specs = (P(("blk", "grp"), None), P(("blk", "grp"), None))
    return jax.shard_map(
        on_device, mesh=mesh, in_specs=in_specs, out_specs=out_specs, check_vma=False
    )
```

profile of v0, /device:TPU:1, one launch (start us, length us, event | category | flops | bytes accessed | tf_op | source)
XLA Modules:
  0.0 1813.5 jit_solution(6392801352030314791)
XLA Ops:
  7.2 0.7 all-gather.7.cloned.1.call-update
  7.9 0.7 all-gather.9.cloned.1.call-update
  8.7 12.4 all_gather.32
  21.1 5.7 all_gather.38
  26.9 1.3 dynamic-slice
  28.1 1.3 dynamic-slice.1
  30.6 206.0 %all-gather.7.cloned.1.call-done = bf16[4096,640]{1,0:T(8,128)(2,1)} async-done(((bf16[32,640]{1,0:T(8,128)(2,1)}), bf16[4096,640]{1,0:T(8,128)(2,1)}) %all-gather.7.cloned.1.call-update) | async-done | bytes 5242896 | tf_op jit(solution)/shard_map/all_gather | solution.py:91
  236.7 38.1 %while.61 = (s32[]{:T(128)}, f32[128]{0:T(128)S(1)}, f32[128]{0:T(128)S(1)}, f32[4096]{0:T(1024)S(1)}, f32[4096]{0:T(1024)S(1)}, /*index=5*/bf16[8,512,640]{2,1,...) while((s32[]{:T(128)}, f32[128]{0:T(128)S(1)}, ...), condition=%wide.region_5.6_spmd.clone, body=%wide.region_0.5_spmd.clone.sunk | while | flops 84344448 | bytes 1364666 | solution.py:83
  236.7 1.5 fusion.86
  241.4 1.5 fusion.86
  246.2 1.5 fusion.86
  251.0 1.5 fusion.86
  255.8 1.5 fusion.86
  260.6 1.5 fusion.86
  265.3 1.5 fusion.86
  270.0 1.5 fusion.86
  274.7 13.9 all-gather.2
  288.6 5.0 all-gather.3
  293.7 595.2 %pmax.7 = f32[4096]{0:T(1024)S(1)} all-reduce(f32[4096]{0:T(1024)S(1)} %get-tuple-element.416), channel_id=1, replica_groups=mesh['blk'=128,'grp'=4] {'blk'}, use_global_device_ids=true, to_apply=%region_6.7 | all-reduce | flops 4096 | bytes 32768 | tf_op jit(solution)/shard_map/pmax | solution.py:85
  889.2 591.7 %all-reduce.2 = (f32[4096]{0:T(1024)S(1)}, f32[4096]{0:T(1024)S(1)}) all-reduce(f32[4096]{0:T(1024)S(1)} %exponential_multiply_fusion, f32[4096]{0:T(1024)S(1)} %dynamic-slice_dynamic-update-slice_fusion.1), channel_id=1, replica_groups=mesh['blk'=128,'grp'=4] {'blk'}, use_global_device_ids=true, to_apply=%region_7.8 | all-reduce | flops 8192 | bytes 65536 | tf_op jit(solution)/shard_map/psum | solution.py:86
  1481.0 224.5 %all-reduce.1 = f32[128]{0:T(128)S(1)} all-reduce(f32[128]{0:T(128)S(1)} %dynamic-slice_dynamic-update-slice_fusion), channel_id=1, replica_groups=mesh['blk'=128,'grp'=4] {'grp'}, use_global_device_ids=true, to_apply=%add.1 | all-reduce | flops 128 | bytes 1024
  1705.5 43.8 %while.62 = (s32[]{:T(128)}, f32[128,640]{1,0:T(8,128)S(1)}, bf16[8,512,640]{2,1,0:T(8,128)(2,1)}, bf16[128,640]{1,0:T(8,128)(2,1)S(1)}, f32[128]{0:T(128)S(1)},...) while((s32[]{:T(128)}, f32[128,640]{1,0:T(8,128)S(1)}, ...), condition=%wide.region_11.12_spmd.clone, body=%wide.region_10.11_spmd.clone.sunk | while | flops 168620160 | bytes 2143428 | solution.py:116
  1708.2 0.7 fusion.92
  1708.8 2.1 fusion.93
  1714.3 2.1 fusion.93
  1719.7 2.2 fusion.93
  1725.3 2.1 fusion.93
  1730.7 2.2 fusion.93
  1736.2 2.1 fusion.93
  1741.0 0.7 fusion.92
  1741.7 2.1 fusion.93
  1746.5 0.7 fusion.92
  1747.1 2.2 fusion.93
  1749.3 0.7 copy-done.1
  1750.1 43.7 %while.63 = (s32[]{:T(128)}, f32[128,640]{1,0:T(8,128)S(1)}, bf16[8,512,640]{2,1,0:T(8,128)(2,1)}, bf16[128,640]{1,0:T(8,128)(2,1)S(1)}, s32[8]{0:T(128)S(1)}, /...) while((s32[]{:T(128)}, f32[128,640]{1,0:T(8,128)S(1)}, ...), condition=%wide.region_14.15_spmd.clone, body=%wide.region_13.14_spmd.clone.sunk | while | flops 168620160 | bytes 2143428 | solution.py:154
  1752.8 0.7 fusion.97
  1753.5 2.1 fusion.98
  1758.2 0.7 fusion.97
  1758.9 2.2 fusion.98
  1763.7 0.7 fusion.97
  1764.4 2.2 fusion.98
  1769.9 2.1 fusion.98
  1775.3 2.1 fusion.98
  1780.8 2.1 fusion.98
  1786.2 2.1 fusion.98
  1791.7 2.1 fusion.98
  1793.8 0.7 copy-done
  1794.6 12.4 reduce-scatter.5.cloned.1.call-done
  (144 shorter events, 29.2 us)
Async XLA Ops:
  7.2 229.5 %all-gather.7.cloned.1.call-start = ((), (), s32[]{:S(2)}) async-start(), calls=%async_computation.2 | async-start | bytes 5283840 | tf_op jit(solution)/shard_map/all_gather | solution.py:91
  7.9 1742.2 %all-gather.9.cloned.1.call-start = ((), (), s32[]{:S(2)}) async-start(), calls=%async_computation.4 | async-start | bytes 5283840 | tf_op jit(solution)/shard_map/all_gather | solution.py:128
  8.6 1785.9 %reduce-scatter.3.cloned.1.call-start = ((), (), s32[]{:S(2)}) async-start(), calls=%async_computation.3 | async-start | bytes 409600 | tf_op jit(solution)/shard_map/reduce_scatter | solution.py:122
  1749.3 0.7 copy-start.1
  1750.1 56.9 %reduce-scatter.5.cloned.1.call-start = ((), (), s32[]{:S(2)}) async-start(), calls=%async_computation.5 | async-start | bytes 409600 | tf_op jit(solution)/shard_map/reduce_scatter | solution.py:159
  1793.8 0.7 copy-start
Sparse Core Ops, SparseCore 0:
  12.5 224.0 all-gather.6
  241.2 222.9 all-gather.8
  1750.2 12.3 reduce-scatter.2
  1794.7 12.2 reduce-scatter.4
where the time goes:
time: 1820 us; the launch traced here: 1810 us
  blocking collectives  1450 us (80%)
  waiting for transfers between devices  220 us (12%)
  loops' own time  46.7 us (3%)
  matrix products  46.5 us (3%)
  local copies, waits for them, and re-layouts  23.9 us (1%)
    pmax x1, blocking collectives, run_sides(): overall_top = lax.pmax(column_top, 'blk')  595 us
    psum x1, blocking collectives, run_sides(): lax.psum(column_mass * jnp.exp(column_top - overall_top), 'blk')  592 us
    unnamed x1, blocking collectives  225 us
    all_gather x1, waiting for transfers between devices, run_sides(): segment = lax.all_gather(other, 'blk', axis=0, tiled=True)  206 us
  transfers between devices with their start and end apart: 4, of which 2 were waited for; matrix products, arithmetic and copies ran while one was open for 5% of the time, Pallas kernels for 0%

commit v1 on v0

v1 whole, which is shorter than its diff:
```python
import jax
import jax.numpy as jnp
from jax import lax
from jax.experimental import pallas as pl
from jax.experimental.pallas import tpu as pltpu
from jax.sharding import PartitionSpec as P

INVERSE_TEMP = 1.0 / 0.07
LOG2E = 1.4426950408889634
MESH = pl.DeviceIdType.MESH
F32 = jnp.float32
BF16 = jnp.bfloat16
D = 640
SHARD = 32
HALF = 16
MOLS = 1024
TEXTS = 512


def place():
    blk, grp = lax.axis_index("blk"), lax.axis_index("grp")
    x = lax.div(blk, 32)
    z = lax.rem(lax.div(blk, 2), 16)
    y = lax.rem(blk, 2) * 2 + lax.div(grp, 2)
    return x, y, lax.div(z, 2), lax.rem(z, 2), lax.rem(grp, 2)


def device(x, y, p, q, c):
    return ((x * 16 + p * 2 + q) * 2 + lax.div(y, 2), lax.rem(y, 2) * 2 + c)


def kernel(
    mol_in, text_in, out,
    mol, text, scores, weights, row_wide, col_top, col_mass, row_part, col_part,
    mol_sum, mol_send, mol_recv1, mol_send2, mol_recv2, mol_send3, mol_recv3,
    text_sum, text_send, text_recv0, text_send1, text_recv1, text_recv2,
    load_sem, pair_sem, mol1_sem, mol2_sem, near_sem, far_sem, sib_sem,
    row_sem, col_sem, rs_sib_sem, rs_text_sem, rs_mol1_sem, rs_mol2_sem, rs_pair_sem,
):
    x, y, p, q, c = place()

    def plus(v, d, n):
        return lax.rem(v + (d + n) % n, n)

    def x_peer(d):
        return device(plus(x, d, 4), y, p, q, c)

    def y_peer(d):
        return device(x, plus(y, d, 4), p, q, c)

    def p_peer(d):
        return device(x, y, plus(p, d, 8), q, c)

    partner = device(x, y, p, 1 - q, c)
    sibling = device(x, y, p, q, 1 - c)

    def send(src, dst, sems, index, target):
        copy = pltpu.make_async_remote_copy(
            src_ref=src,
            dst_ref=dst,
            send_sem=sems.at[(0,) + index],
            recv_sem=sems.at[(1,) + index],
            device_id=target,
            device_id_type=MESH,
        )
        copy.start()
        return copy

    started = []

    def rows(start, size):
        return pl.ds(pl.multiple_of(start, 16), size)

    def mol_row(h, x_, y_):
        return (y_ * 4 + x_) * SHARD if h == 0 else MOLS // 2 + (x_ * 4 + y_) * SHARD

    def text_row(p_, c_):
        return (c_ * 8 + p_) * SHARD

    own_row = [mol_row(0, x, y) + q * HALF, mol_row(1, x, y) + q * HALF]
    partner_row = [mol_row(0, x, y) + (1 - q) * HALF, mol_row(1, x, y) + (1 - q) * HALF]
    loads = [
        pltpu.make_async_copy(mol_in.at[pl.ds(0, HALF)], mol.at[rows(own_row[0], HALF)], load_sem.at[0]),
        pltpu.make_async_copy(mol_in.at[pl.ds(HALF, HALF)], mol.at[rows(own_row[1], HALF)], load_sem.at[1]),
        pltpu.make_async_copy(text_in, text.at[rows(text_row(p, c), SHARD)], load_sem.at[2]),
    ]
    for load in loads:
        load.start()

    peers = [p_peer(d) for d in (1, -1, 2, -2)] + [partner, sibling]
    peers += [x_peer(d) for d in (1, 2, 3)] + [y_peer(d) for d in (1, 2, 3)]
    barrier = pltpu.get_barrier_semaphore()
    for peer in peers:
        pl.semaphore_signal(barrier, inc=1, device_id=peer, device_id_type=MESH)
    pl.semaphore_wait(barrier, len(peers))
    for load in loads:
        load.wait()

    def text_send_rows(p_, c_, sems, index, target, first=0, size=SHARD):
        block = text.at[rows(text_row(p_, c_) + first, size)]
        copy = send(block, block, sems, index, target)
        started.append(copy)
        return copy

    def mol_send_rows(start, size, sems, index, target):
        block = mol.at[rows(start, size)]
        copy = send(block, block, sems, index, target)
        started.append(copy)
        return copy

    first_peer = [x_peer, y_peer]
    second_peer = [y_peer, x_peer]
    two = {d: text_send_rows(p, c, near_sem, (i,), p_peer(d)) for i, d in ((0, 2), (1, -2))}
    pair = [mol_send_rows(own_row[h], HALF, pair_sem, (h,), partner) for h in (0, 1)]
    stage1 = {}
    for d in (1, 3, 2):
        for h in (0, 1):
            stage1[h, 0, d] = mol_send_rows(own_row[h], HALF, mol1_sem, (h, 0, d), first_peer[h](d))
    one = {d: text_send_rows(p, c, near_sem, (i,), p_peer(d)) for i, d in ((2, 1), (3, -1))}
    sib = [text_send_rows(p, c, sib_sem, (0,), sibling)]
    for h in (0, 1):
        pair[h].wait_recv()
    for d in (1, 3, 2):
        for h in (0, 1):
            stage1[h, 1, d] = mol_send_rows(partner_row[h], HALF, mol1_sem, (h, 1, d), first_peer[h](d))
    stage2 = []

    def spread(e):
        xe, ye = plus(x, e, 4), plus(y, e, 4)
        starts = [mol_row(0, xe, y), mol_row(1, x, ye)]
        for d in (1, 3, 2):
            for h in (0, 1):
                stage2.append(mol_send_rows(starts[h], SHARD, mol2_sem, (h, e, d), second_peer[h](d)))

    spread(0)
    for e in (1, 3):
        for h in (0, 1):
            stage1[h, 0, (4 - e) % 4].wait_recv()
            stage1[h, 1, (4 - e) % 4].wait_recv()
        spread(e)
    far = []
    for i, d in ((0, 2), (1, -2)):
        two[d].wait_recv()
        back = plus(p, -d, 8)
        far.append(text_send_rows(back, c, far_sem, (2 + i,), p_peer(d), i * HALF, HALF))
        far.append(text_send_rows(back, c, far_sem, (i,), p_peer(d // 2)))
        sib.append(text_send_rows(back, c, sib_sem, (1 + i,), sibling))
    for h in (0, 1):
        stage1[h, 0, 2].wait_recv()
        stage1[h, 1, 2].wait_recv()
    spread(2)
    for i, d in ((3, 1), (4, -1)):
        one[d].wait_recv()
        sib.append(text_send_rows(plus(p, -d, 8), c, sib_sem, (i,), sibling))
    for copy in far:
        copy.wait_recv()
    sib.append(text_send_rows(plus(p, 3, 8), c, sib_sem, (5,), sibling))
    sib.append(text_send_rows(plus(p, -3, 8), c, sib_sem, (6,), sibling))
    sib.append(text_send_rows(plus(p, 4, 8), c, sib_sem, (7,), sibling))
    for copy in stage2:
        copy.wait_recv()
    for copy in sib:
        copy.wait_recv()

    scores[...] = lax.dot_general(
        mol[...], text[...], (((1,), (1,)), ((), ())), preferred_element_type=F32
    ) * (INVERSE_TEMP * LOG2E)
    row_me = (x * 4 + y) * 2 + q
    col_me = c * 8 + p
    lanes = [slice(128 * k, 128 * k + 128) for k in range(TEXTS // 128)]

    def totals(b, carry):
        block = pl.ds(pl.multiple_of(b * 128, 128), 128)
        parts = [scores[block, lane] for lane in lanes]
        top = jnp.maximum(jnp.maximum(parts[0], parts[1]), jnp.maximum(parts[2], parts[3]))
        mass = sum(jnp.exp2(part - top) for part in parts)
        top, mass = top.T, mass.T
        overall = jnp.max(top, axis=0, keepdims=True)
        mass = jnp.sum(mass * jnp.exp2(top - overall), axis=0, keepdims=True)
        row_part[row_me, pl.ds(b, 1), :] = overall + jnp.log2(mass)
        for part, lane in zip(parts, lanes):
            tiles = part.reshape(16, 8, 128)
            top = jnp.max(tiles, axis=0)
            col_top[b, :, lane] = top
            col_mass[b, :, lane] = jnp.sum(jnp.exp2(tiles - top[None]), axis=0)
        return carry

    lax.fori_loop(0, MOLS // 128, totals, 0)
    for k, lane in enumerate(lanes):
        top = col_top[:, :, lane].reshape(64, 128)
        overall = jnp.max(top, axis=0, keepdims=True)
        mass = jnp.sum(col_mass[:, :, lane].reshape(64, 128) * jnp.exp2(top - overall), axis=0, keepdims=True)
        col_part[col_me, pl.ds(k, 1), :] = overall + jnp.log2(mass)

    exchange = []
    for d in (4, 3, 5, 2, 6, 1, 7, 0):
        for e in (0, 1):
            if d or e:
                block = col_part.at[col_me, pl.ds(0, 4)]
                target = device(x, y, plus(p, d, 8), q, c if e == 0 else 1 - c)
                exchange.append(send(block, block, col_sem, (d * 2 + e,), target))
    for dx in (2, 1, 3, 0):
        for dy in (2, 1, 3, 0):
            for e in (0, 1):
                if dx or dy or e:
                    block = row_part.at[row_me]
                    target = device(plus(x, dx, 4), plus(y, dy, 4), p, q if e == 0 else 1 - q, c)
                    exchange.append(send(block, block, row_sem, ((dx * 4 + dy) * 2 + e,), target))
    for copy in exchange:
        copy.wait_recv()
    started.extend(exchange)

    def merge(parts):
        top = jnp.max(parts, axis=0)
        return top + jnp.log2(jnp.sum(jnp.exp2(parts - top[None]), axis=0))

    row_lse = merge(row_part[...])
    col_lse = merge(col_part[:, 0:4, :])

    for b in range(MOLS // 128):
        row_wide[128 * b : 128 * b + 128, :] = jnp.broadcast_to(row_lse[b : b + 1, :], (128, 128)).T

    def weigh(part, row, k):
        return 0.5 * jnp.exp2(part - row) + 0.5 * jnp.exp2(part - col_lse[k : k + 1, :])

    def weight(b, carry):
        block = pl.ds(pl.multiple_of(b * 128, 128), 128)
        row = row_wide[block, :]
        for k, lane in enumerate(lanes):
            weights[block, lane] = weigh(scores[block, lane], row, k).astype(BF16)
        return carry

    lax.fori_loop(0, MOLS // 128, weight, 0)
    for h in (0, 1):
        block = rows(own_row[h], HALF)
        row = row_wide[block, :]
        ahead = lax.broadcasted_iota(jnp.int32, (HALF, 128), 1) - lax.broadcasted_iota(jnp.int32, (HALF, 128), 0)
        for k, lane in enumerate(lanes):
            paired = (ahead == text_row(p, c) + h * HALF - 128 * k).astype(F32)
            weights[block, lane] = (weigh(scores[block, lane], row, k) - paired).astype(BF16)

    text_sum[...] = lax.dot_general(
        weights[...], mol[...], (((0,), (0,)), ((), ())), preferred_element_type=F32
    )
    other = rows((1 - c) * (TEXTS // 2), TEXTS // 2)
    text_send[...] = text_sum[other, :].astype(BF16)
    rs_sib = send(text_send, text_recv0, rs_sib_sem, (0,), sibling)
    started.append(rs_sib)

    mol_sum[...] = jnp.dot(weights[...], text[...], preferred_element_type=F32)
    mol_send[...] = mol_sum[...].astype(BF16)
    quarter = 4 * SHARD
    rs_mol1 = {}
    for d in (2, 1, 3):
        for h in (0, 1):
            there = (plus(y, d, 4) if h == 0 else plus(x, d, 4)) * quarter + h * (MOLS // 2)
            rs_mol1[h, d] = send(
                mol_send.at[rows(there, quarter)], mol_recv1.at[h, d], rs_mol1_sem, (h, d), second_peer[h](d)
            )
            started.append(rs_mol1[h, d])

    rs_sib.wait_recv()
    mine = rows(c * (TEXTS // 2), TEXTS // 2)
    text_sum[mine, :] = text_sum[mine, :] + text_recv0[...].astype(F32)
    rs_text = {}

    def text_block(d):
        return text_sum[rows(text_row(plus(p, d, 8), c), SHARD), :]

    for i, d in enumerate((3, -3, 4, 1, -1)):
        text_send1[i] = text_block(d).astype(BF16)
    rs_text["4a"] = send(
        text_send1.at[2, pl.ds(0, HALF)], text_recv1.at[2, pl.ds(0, HALF)], rs_text_sem, (2,), p_peer(2)
    )
    rs_text["4b"] = send(
        text_send1.at[2, pl.ds(HALF, HALF)], text_recv1.at[2, pl.ds(HALF, HALF)], rs_text_sem, (3,), p_peer(-2)
    )
    rs_text[3] = send(text_send1.at[0], text_recv1.at[0], rs_text_sem, (0,), p_peer(1))
    rs_text[-3] = send(text_send1.at[1], text_recv1.at[1], rs_text_sem, (1,), p_peer(-1))
    rs_text[1] = send(text_send1.at[3], text_recv2.at[0], rs_text_sem, (4,), p_peer(1))
    rs_text[-1] = send(text_send1.at[4], text_recv2.at[1], rs_text_sem, (5,), p_peer(-1))

    rs_mol2 = {}
    for h in (0, 1):
        base = (y if h == 0 else x) * quarter + h * (MOLS // 2)
        for d in (1, 3, 2):
            rs_mol1[h, d].wait_recv()
        block = mol_sum[rows(base, quarter), :]
        for d in (1, 2, 3):
            block = block + mol_recv1[h, d].astype(F32)
        mol_sum[rows(base, quarter), :] = block
        for d in (2, 1, 3):
            there = base + (plus(x, d, 4) if h == 0 else plus(y, d, 4)) * SHARD
            mol_send2[h, d] = mol_sum[rows(there, SHARD), :].astype(BF16)
            rs_mol2[h, d] = send(mol_send2.at[h, d], mol_recv2.at[h, d], rs_mol2_sem, (h, d), first_peer[h](d))

    for name in ("4a", "4b", 3, -3):
        rs_text[name].wait_recv()
    ahead = text_block(2) + text_recv1[0].astype(F32)
    text_send1[5, pl.ds(0, HALF)] = (ahead[:HALF] + text_recv1[2, pl.ds(0, HALF)].astype(F32)).astype(BF16)
    text_send1[5, pl.ds(HALF, HALF)] = ahead[HALF:].astype(BF16)
    rs_text[2] = send(text_send1.at[5], text_recv2.at[2], rs_text_sem, (6,), p_peer(2))
    behind = text_block(-2) + text_recv1[1].astype(F32)
    text_send1[6, pl.ds(0, HALF)] = behind[:HALF].astype(BF16)
    text_send1[6, pl.ds(HALF, HALF)] = (behind[HALF:] + text_recv1[2, pl.ds(HALF, HALF)].astype(F32)).astype(BF16)
    rs_text[-2] = send(text_send1.at[6], text_recv2.at[3], rs_text_sem, (7,), p_peer(-2))

    rs_pair = []
    for h in (0, 1):
        for d in (1, 3, 2):
            rs_mol2[h, d].wait_recv()
        here = mol_row(h, x, y)
        block = mol_sum[rows(here, SHARD), :]
        for d in (1, 2, 3):
            block = block + mol_recv2[h, d].astype(F32)
        mol_sum[rows(here, SHARD), :] = block
        mol_send3[h] = mol_sum[rows(partner_row[h], HALF), :].astype(BF16)
        rs_pair.append(send(mol_send3.at[h], mol_recv3.at[h], rs_pair_sem, (h,), partner))
    for h in (0, 1):
        rs_pair[h].wait_recv()
        out[0, pl.ds(HALF * h, HALF), :] = (
            mol_sum[rows(own_row[h], HALF), :] + mol_recv3[h].astype(F32)
        ) * INVERSE_TEMP
    total = text_block(0)
    for i, d in enumerate((1, -1, 2, -2)):
        rs_text[d].wait_recv()
        total = total + text_recv2[i].astype(F32)
    out[1] = total * INVERSE_TEMP

    started.extend(rs_text.values())
    started.extend(rs_mol2.values())
    started.extend(rs_pair)
    for copy in started:
        copy.wait_send()


def on_device(molecules, texts):
    dma = pltpu.SemaphoreType.DMA
    both = pl.pallas_call(
        kernel,
        out_shape=jax.ShapeDtypeStruct((2, SHARD, D), F32),
        in_specs=[pl.BlockSpec(memory_space=pl.ANY)] * 2,
        out_specs=pl.BlockSpec(memory_space=pltpu.VMEM),
        scratch_shapes=[
            pltpu.VMEM((MOLS, D), BF16),
            pltpu.VMEM((TEXTS, D), BF16),
            pltpu.VMEM((MOLS, TEXTS), F32),
            pltpu.VMEM((MOLS, TEXTS), BF16),
            pltpu.VMEM((MOLS, 128), F32),
            pltpu.VMEM((8, 8, TEXTS), F32),
            pltpu.VMEM((8, 8, TEXTS), F32),
            pltpu.VMEM((32, 8, 128), F32),
            pltpu.VMEM((16, 8, 128), F32),
            pltpu.VMEM((MOLS, D), F32),
            pltpu.VMEM((MOLS, D), BF16),
            pltpu.VMEM((2, 4, 4 * SHARD, D), BF16),
            pltpu.VMEM((2, 4, SHARD, D), BF16),
            pltpu.VMEM((2, 4, SHARD, D), BF16),
            pltpu.VMEM((2, HALF, D), BF16),
            pltpu.VMEM((2, HALF, D), BF16),
            pltpu.VMEM((TEXTS, D), F32),
            pltpu.VMEM((TEXTS // 2, D), BF16),
            pltpu.VMEM((TEXTS // 2, D), BF16),
            pltpu.VMEM((7, SHARD, D), BF16),
            pltpu.VMEM((3, SHARD, D), BF16),
            pltpu.VMEM((4, SHARD, D), BF16),
            dma((3,)),
            dma((2, 2)),
            dma((2, 2, 2, 4)),
            dma((2, 2, 4, 4)),
            dma((2, 4)),
            dma((2, 4)),
            dma((2, 8)),
            dma((2, 32)),
            dma((2, 16)),
            dma((2, 1)),
            dma((2, 8)),
            dma((2, 2, 4)),
            dma((2, 2, 4)),
            dma((2, 2)),
        ],
        compiler_params=pltpu.CompilerParams(
            collective_id=0, has_side_effects=True, vmem_limit_bytes=40 << 20
        ),
    )(molecules, texts)
    return both[0], both[1]


def solution(mesh):
    spec = P(("blk", "grp"), None)
    return jax.shard_map(
        on_device, mesh=mesh, in_specs=(spec, spec), out_specs=(spec, spec), check_vma=False
    )
```

time: 1820 us -> 68.1 us (0.04)
  blocking collectives: 1450 us -> 0 us
  waiting for transfers between devices: 220 us -> 0 us
  Pallas kernels: 0 us -> 65 us
  loops' own time: 46.7 us -> 0 us
  matrix products: 46.5 us -> 0 us
  local copies, waits for them, and re-layouts: 23.9 us -> 2.22 us
    pmax x1 -> x0, blocking collectives: 595 us -> none  [run_sides(): overall_top = lax.pmax(column_top, 'blk')]
    psum x1 -> x0, blocking collectives: 592 us -> none  [run_sides(): lax.psum(column_mass * jnp.exp(column_top - overall_top), 'blk')]
    unnamed x1 -> x0, blocking collectives: 225 us -> none
    all_gather x2 -> x0, waiting for transfers between devices: 206 us -> none  [the longest x1 206 us: run_sides(): segment = lax.all_gather(other, 'blk', axis=0, tiled=True)]
    pallas_call x0 -> x1, Pallas kernels: none -> 65 us  [on_device(): pl.pallas_call(kernel, out_shape=jax.ShapeDtypeStruct((2, SHARD, D), F32)...]
    another operation x4 -> x0, loops' own time: 46.7 us -> none  [the longest x1 15.8 us: run_sides(): lax.scan(other_advance, jnp.zeros((height, features), jnp.float32), (spli...]
    dot_general x24 -> x0, matrix products: 46.5 us -> none  [the longest x8 17.3 us: grad_advance(): jnp.dot(weights, other_block, preferred_element_type=jnp.float32)]
    all_gather x4 -> x0, blocking collectives: 37.1 us -> none  [the longest x2 18.9 us: merged(): everything = jax.tree.map(lambda part: lax.all_gather(part, axis), x)]
  transfers between devices with their start and end apart: 4 -> 0, of which waited for: 2 -> 0; matrix products, arithmetic and copies ran while one was open for 5% -> 0% of each run, Pallas kernels for 0% -> 0%
where the time goes in v1:
time: 68.1 us; the launch traced here: 67.8 us
  Pallas kernels  65 us (95%)
  local copies, waits for them, and re-layouts  2.22 us (3%)
    pallas_call x1, Pallas kernels, on_device(): pl.pallas_call(kernel, out_shape=jax.ShapeDtypeStruct((2, SHARD, D), F32)...  65 us
    unnamed x4, local copies, waits for them, and re-layouts  1.55 us

profile of v1, /device:TPU:1, one launch (start us, length us, event | category | flops | bytes accessed | tf_op | source)
XLA Modules:
  0.0 67.8 jit_solution(10540055420022217425)
XLA Ops:
  0.6 0.0 copy-start
  0.6 0.8 %copy-done = bf16[32,640]{1,0:T(8,128)(2,1)S(1)} copy-done((bf16[32,640]{1,0:T(8,128)(2,1)S(1)}, bf16[32,640]{1,0:T(8,128)(2,1)}, u32[]{:S(2)}) %copy-start) | copy-done | bytes 40984
  1.4 0.0 copy-start.1
  1.4 0.8 %copy-done.1 = bf16[32,640]{1,0:T(8,128)(2,1)S(1)} copy-done((bf16[32,640]{1,0:T(8,128)(2,1)S(1)}, bf16[32,640]{1,0:T(8,128)(2,1)}, u32[]{:S(2)}) %copy-start.1) | copy-done | bytes 40984
  2.2 65.0 %shard_map.41 = f32[2,32,640]{2,1,0:T(8,128)S(1)} custom-call(bf16[32,640]{1,0:T(8,128)(2,1)S(1)} %copy-done, bf16[32,640]{1,0:T(8,128)(2,1)S(1)} %copy-done.1), custom_call_target="tpu_custom_call" | custom-call | tf_op jit(solution)/shard_map/pallas_call | solution.py:339
  67.2 0.7 slice_bitcast_fusion
Async XLA Ops:
  0.6 0.8 %copy-start = (bf16[32,640]{1,0:T(8,128)(2,1)S(1)}, bf16[32,640]{1,0:T(8,128)(2,1)}, u32[]{:S(2)}) copy-start(bf16[32,640]{1,0:T(8,128)(2,1)} %mol_in.1) | copy-start | bytes 122884
  1.4 0.8 %copy-start.1 = (bf16[32,640]{1,0:T(8,128)(2,1)S(1)}, bf16[32,640]{1,0:T(8,128)(2,1)}, u32[]{:S(2)}) copy-start(bf16[32,640]{1,0:T(8,128)(2,1)} %text_in.1) | copy-start | bytes 122884

commit v2 on v1

v2 whole, which is shorter than its diff:
```python
import jax
import jax.numpy as jnp
from jax import lax
from jax.experimental import pallas as pl
from jax.experimental.pallas import tpu as pltpu
from jax.sharding import PartitionSpec as P

INVERSE_TEMP = 1.0 / 0.07
LOG2E = 1.4426950408889634
MESH = pl.DeviceIdType.MESH
F32 = jnp.float32
BF16 = jnp.bfloat16
D = 640
SHARD = 32
HALF = 16
MOLS = 1024
TEXTS = 512


def place():
    blk, grp = lax.axis_index("blk"), lax.axis_index("grp")
    x = lax.div(blk, 32)
    z = lax.rem(lax.div(blk, 2), 16)
    y = lax.rem(blk, 2) * 2 + lax.div(grp, 2)
    return x, y, lax.div(z, 2), lax.rem(z, 2), lax.rem(grp, 2)


def device(x, y, p, q, c):
    return ((x * 16 + p * 2 + q) * 2 + lax.div(y, 2), lax.rem(y, 2) * 2 + c)


def kernel(
    mol_in, text_in, out,
    mol, text, scores, by_row, weights, row_wide, col_top, col_mass, row_part, col_part,
    mol_sum, mol_send, mol_recv1, mol_send2, mol_recv2, mol_send3, mol_recv3,
    text_sum, text_send, text_recv0, text_send1, text_recv1,
    sent_sem, load_sem, pair_sem, mol1_sem, mol2_sem, near_sem, far_sem, sib_sem, row_sem, col_sem,
    rs_sib_sem, rs_text_sem, rs_mol1_sem, rs_mol2_sem, rs_pair_sem,
):
    x, y, p, q, c = place()

    def plus(v, d, n):
        return lax.rem(v + (d + n) % n, n)

    def x_peer(d):
        return device(plus(x, d, 4), y, p, q, c)

    def y_peer(d):
        return device(x, plus(y, d, 4), p, q, c)

    def p_peer(d):
        return device(x, y, plus(p, d, 8), q, c)

    partner = device(x, y, p, 1 - q, c)
    sibling = device(x, y, p, q, 1 - c)

    def send(src, dst, phase, sem, target):
        pltpu.make_async_remote_copy(
            src_ref=src,
            dst_ref=dst,
            send_sem=sent_sem.at[phase],
            recv_sem=sem,
            device_id=target,
            device_id_type=MESH,
        ).start()

    def await_bytes(ref, sem):
        pltpu.make_async_copy(ref, ref, sem).wait()

    def await_rows(count, sem):
        await_bytes(mol_sum.at[pl.ds(0, count // 2)], sem)

    def rows(start, size):
        return pl.ds(pl.multiple_of(start, 16), size)

    def mol_row(h, q_, x_, y_):
        return h * (MOLS // 2) + q_ * (MOLS // 4) + (y_ * 4 + x_ if h == 0 else x_ * 4 + y_) * HALF

    def text_row(p_, c_):
        return (c_ * 8 + p_) * SHARD

    other_q = 1 - q
    own_row = [mol_row(h, q, x, y) for h in (0, 1)]
    partner_row = [mol_row(h, other_q, x, y) for h in (0, 1)]
    loads = [
        pltpu.make_async_copy(mol_in.at[pl.ds(0, HALF)], mol.at[rows(own_row[0], HALF)], load_sem.at[0]),
        pltpu.make_async_copy(mol_in.at[pl.ds(HALF, HALF)], mol.at[rows(own_row[1], HALF)], load_sem.at[0]),
        pltpu.make_async_copy(text_in, text.at[rows(text_row(p, c), SHARD)], load_sem.at[0]),
    ]
    for load in loads:
        load.start()

    peers = [p_peer(d) for d in (1, -1, 2, -2)] + [partner, sibling]
    peers += [x_peer(d) for d in (1, 2, 3)] + [y_peer(d) for d in (1, 2, 3)]
    barrier = pltpu.get_barrier_semaphore()
    for peer in peers:
        pl.semaphore_signal(barrier, inc=1, device_id=peer, device_id_type=MESH)
    pl.semaphore_wait(barrier, len(peers))
    await_rows(2 * SHARD, load_sem.at[0])

    def text_send_rows(p_, c_, sem, target, first=0, size=SHARD):
        block = text.at[rows(text_row(p_, c_) + first, size)]
        send(block, block, 0, sem, target)

    def mol_send_rows(start, size, sem, target):
        block = mol.at[rows(start, size)]
        send(block, block, 0, sem, target)

    first_peer = [x_peer, y_peer]
    second_peer = [y_peer, x_peer]
    low, high = (0, HALF), (HALF, HALF)

    def fan(own):
        for d in (1, 3, 2):
            for h in (0, 1):
                start = own_row[h] if own else partner_row[h]
                mol_send_rows(start, HALF, mol1_sem.at[own, d], first_peer[h](d))

    def spread(own, e):
        q_ = q if own else other_q
        starts = [mol_row(0, q_, plus(x, e, 4), y), mol_row(1, q_, x, plus(y, e, 4))]
        for d in (1, 3, 2):
            for h in (0, 1):
                mol_send_rows(starts[h], HALF, mol2_sem.at[0], second_peer[h](d))

    def fan_arrived(own, e):
        await_rows(2 * HALF, mol1_sem.at[own, 4 - e])

    def to_sibling(d):
        text_send_rows(plus(p, d, 8), c, sib_sem.at[0], sibling)

    for h in (0, 1):
        mol_send_rows(own_row[h], HALF, pair_sem.at[0], partner)
    for i, (d, part) in enumerate(((2, low), (-2, high), (2, high), (-2, low))):
        text_send_rows(p, c, near_sem.at[i], p_peer(d), *part)
    fan(1)
    spread(1, 0)
    for d in (1, -1):
        text_send_rows(p, c, near_sem.at[4], p_peer(d))
    to_sibling(0)
    await_rows(2 * HALF, pair_sem.at[0])
    fan(0)
    spread(0, 0)
    for e in (1, 3, 2):
        fan_arrived(1, e)
        spread(1, e)

    def forward(i, source, d, part):
        text_send_rows(plus(p, source, 8), c, far_sem.at[i], p_peer(d), *part)

    await_rows(HALF, near_sem.at[0])
    forward(0, -2, 2, low)
    forward(1, -2, 1, low)
    await_rows(HALF, near_sem.at[1])
    forward(0, 2, -2, high)
    forward(1, 2, -1, high)
    for e in (1, 3, 2):
        fan_arrived(0, e)
        spread(0, e)
    await_rows(HALF, near_sem.at[2])
    forward(1, -2, 1, high)
    to_sibling(-2)
    await_rows(HALF, near_sem.at[3])
    forward(1, 2, -1, low)
    to_sibling(2)
    await_rows(2 * SHARD, near_sem.at[4])
    to_sibling(-1)
    to_sibling(1)
    await_rows(2 * SHARD, far_sem.at[1])
    to_sibling(-3)
    to_sibling(3)
    await_rows(SHARD, far_sem.at[0])
    to_sibling(4)
    await_rows(48 * HALF, mol2_sem.at[0])
    await_rows(8 * SHARD, sib_sem.at[0])
    await_rows(1472, sent_sem.at[0])

    scores[...] = lax.dot_general(
        mol[...], text[...], (((1,), (1,)), ((), ())), preferred_element_type=F32
    ) * (INVERSE_TEMP * LOG2E)
    row_me = (x * 4 + y) * 2 + q
    col_me = c * 8 + p
    lanes = [slice(128 * k, 128 * k + 128) for k in range(TEXTS // 128)]

    def column_totals(b, carry):
        for lane in lanes:
            tiles = scores[pl.ds(pl.multiple_of(b * 128, 128), 128), lane].reshape(16, 8, 128)
            top = jnp.max(tiles, axis=0)
            col_top[b, :, lane] = top
            col_mass[b, :, lane] = jnp.sum(jnp.exp2(tiles - top[None]), axis=0)
        return carry

    lax.fori_loop(0, MOLS // 128, column_totals, 0)
    for k, lane in enumerate(lanes):
        top = col_top[:, :, lane].reshape(64, 128)
        overall = jnp.max(top, axis=0, keepdims=True)
        mass = jnp.sum(col_mass[:, :, lane].reshape(64, 128) * jnp.exp2(top - overall), axis=0, keepdims=True)
        col_part[col_me, pl.ds(k, 1), :] = overall + jnp.log2(mass)
    for d in (4, 3, 5, 2, 6, 1, 7, 0):
        for e in (0, 1):
            if d or e:
                block = col_part.at[col_me, pl.ds(0, 4)]
                target = device(x, y, plus(p, d, 8), q, c if e == 0 else 1 - c)
                send(block, block, 1, col_sem.at[0], target)

    def row_totals(b, carry):
        block = pl.ds(pl.multiple_of(b * 128, 128), 128)
        parts = [scores[block, lane] for lane in lanes]
        top = jnp.maximum(jnp.maximum(parts[0], parts[1]), jnp.maximum(parts[2], parts[3]))
        mass = sum(jnp.exp2(part - top) for part in parts)
        top, mass = top.T, mass.T
        overall = jnp.max(top, axis=0, keepdims=True)
        mass = jnp.sum(mass * jnp.exp2(top - overall), axis=0, keepdims=True)
        row_part[row_me, pl.ds(b, 1), :] = overall + jnp.log2(mass)
        return carry

    lax.fori_loop(0, MOLS // 128, row_totals, 0)
    for dx in (2, 1, 3, 0):
        for dy in (2, 1, 3, 0):
            for e in (0, 1):
                if dx or dy or e:
                    block = row_part.at[row_me]
                    target = device(plus(x, dx, 4), plus(y, dy, 4), p, q if e == 0 else other_q, c)
                    send(block, block, 2, row_sem.at[0], target)

    def merge(parts):
        top = jnp.max(parts, axis=0)
        return top + jnp.log2(jnp.sum(jnp.exp2(parts - top[None]), axis=0))

    await_bytes(row_part.at[pl.ds(0, 31)], row_sem.at[0])
    row_lse = merge(row_part[...])
    for b in range(MOLS // 128):
        row_wide[128 * b : 128 * b + 128, :] = jnp.broadcast_to(row_lse[b : b + 1, :], (128, 128)).T

    def row_weight(b, carry):
        block = pl.ds(pl.multiple_of(b * 128, 128), 128)
        row = row_wide[block, :]
        for lane in lanes:
            by_row[block, lane] = 0.5 * jnp.exp2(scores[block, lane] - row)
        return carry

    lax.fori_loop(0, MOLS // 128, row_weight, 0)
    await_bytes(col_part.at[pl.ds(0, 15), pl.ds(0, 4)], col_sem.at[0])
    col_lse = merge(col_part[:, 0:4, :])

    def weigh(block, k):
        lane = lanes[k]
        return by_row[block, lane] + 0.5 * jnp.exp2(scores[block, lane] - col_lse[k : k + 1, :])

    def weight(b, carry):
        block = pl.ds(pl.multiple_of(b * 128, 128), 128)
        for k, lane in enumerate(lanes):
            weights[block, lane] = weigh(block, k).astype(BF16)
        return carry

    lax.fori_loop(0, MOLS // 128, weight, 0)
    for h in (0, 1):
        block = rows(own_row[h], HALF)
        ahead = lax.broadcasted_iota(jnp.int32, (HALF, 128), 1) - lax.broadcasted_iota(jnp.int32, (HALF, 128), 0)
        for k, lane in enumerate(lanes):
            paired = (ahead == text_row(p, c) + h * HALF - 128 * k).astype(F32)
            weights[block, lane] = (weigh(block, k) - paired).astype(BF16)

    def text_part(c_):
        lane = pl.ds(pl.multiple_of(c_ * (TEXTS // 2), TEXTS // 2), TEXTS // 2)
        return lax.dot_general(weights[:, lane], mol[...], (((0,), (0,)), ((), ())), preferred_element_type=F32)

    text_send[...] = text_part(1 - c).astype(BF16)
    send(text_send, text_recv0, 3, rs_sib_sem.at[0], sibling)
    text_sum[...] = text_part(c)

    def mol_parts(own):
        for h in (0, 1):
            block = rows(h * (MOLS // 2) + (q if own else other_q) * (MOLS // 4), MOLS // 4)
            part = jnp.dot(weights[block, :], text[...], preferred_element_type=F32)
            mol_sum[block, :] = part
            mol_send[block, :] = part.astype(BF16)
        q_ = q if own else other_q
        for e in (2, 1, 3, 0):
            starts = {}
            for d in (2, 1, 3):
                starts[0, d] = mol_row(0, q_, plus(x, e, 4), plus(y, d, 4))
                starts[1, d] = mol_row(1, q_, plus(x, d, 4), plus(y, e, 4))
            for d in (2, 1, 3):
                for h in (0, 1):
                    send(
                        mol_send.at[rows(starts[h, d], HALF)],
                        mol_recv1.at[h, own, e, d],
                        3,
                        rs_mol1_sem.at[own, e],
                        second_peer[h](d),
                    )

    mol_parts(0)

    await_rows(TEXTS // 2, rs_sib_sem.at[0])
    text_sum[...] = text_sum[...] + text_recv0[...].astype(F32)

    def text_block(d, part=(0, SHARD)):
        return text_sum[pl.ds(pl.multiple_of(plus(p, d, 8) * SHARD + part[0], HALF), part[1]), :]

    for slot, d in enumerate((4, 3, -3, 1, -1)):
        text_send1[slot] = text_block(d).astype(BF16)

    def text_pass(i, slot, part, d):
        span = pl.ds(part[0], part[1])
        send(text_send1.at[slot, span], text_recv1.at[slot, span], 3, rs_text_sem.at[i], p_peer(d))

    text_pass(1, 0, low, 2)
    text_pass(1, 0, high, -2)
    text_pass(0, 1, high, 1)
    text_pass(0, 2, low, -1)
    text_pass(1, 1, low, 1)
    text_pass(1, 2, high, -1)
    text_pass(2, 3, (0, SHARD), 1)
    text_pass(2, 4, (0, SHARD), -1)

    mol_parts(1)

    def text_pass2(d, part, *arrived):
        total = text_block(d, part)
        for slot in arrived:
            total = total + text_recv1[slot, pl.ds(*part), :].astype(F32)
        slot = 5 if d > 0 else 6
        text_send1[slot, pl.ds(*part), :] = total.astype(BF16)
        text_pass(2, slot, part, d)

    def mol_pass2(own, e):
        q_ = q if own else other_q
        await_rows(6 * HALF, rs_mol1_sem.at[own, e])
        for h in (0, 1):
            start = mol_row(0, q_, plus(x, e, 4), y) if h == 0 else mol_row(1, q_, x, plus(y, e, 4))
            block = mol_sum[rows(start, HALF), :]
            for d in (2, 1, 3):
                block = block + mol_recv1[h, own, e, d].astype(F32)
            if e == 0:
                mol_sum[rows(start, HALF), :] = block
            else:
                mol_send2[h, own, e] = block.astype(BF16)
                send(mol_send2.at[h, own, e], mol_recv2.at[h, own, e], 3, rs_mol2_sem.at[own], first_peer[h](e))

    def mol_total(own, h):
        block = mol_sum[rows(own_row[h] if own else partner_row[h], HALF), :]
        for d in (1, 3, 2):
            block = block + mol_recv2[h, own, d].astype(F32)
        return block

    mol_pass2(0, 2)
    await_rows(SHARD, rs_text_sem.at[0])
    text_pass2(2, high, 1)
    text_pass2(-2, low, 2)
    mol_pass2(0, 1)
    mol_pass2(0, 3)
    await_rows(2 * SHARD, rs_text_sem.at[1])
    text_pass2(2, low, 1, 0)
    text_pass2(-2, high, 2, 0)
    mol_pass2(0, 0)
    mol_pass2(1, 2)
    mol_pass2(1, 1)
    await_rows(6 * HALF, rs_mol2_sem.at[0])
    for h in (0, 1):
        mol_send3[h] = mol_total(0, h).astype(BF16)
        send(mol_send3.at[h], mol_recv3.at[h], 3, rs_pair_sem.at[0], partner)
    mol_pass2(1, 3)
    mol_pass2(1, 0)
    await_rows(4 * SHARD, rs_text_sem.at[2])
    total = text_block(0)
    for slot in (3, 4, 5, 6):
        total = total + text_recv1[slot].astype(F32)
    out[1] = total * INVERSE_TEMP
    await_rows(6 * HALF, rs_mol2_sem.at[1])
    await_rows(2 * HALF, rs_pair_sem.at[0])
    for h in (0, 1):
        out[0, pl.ds(HALF * h, HALF), :] = (mol_total(1, h) + mol_recv3[h].astype(F32)) * INVERSE_TEMP

    await_bytes(col_part.at[pl.ds(0, 15), pl.ds(0, 4)], sent_sem.at[1])
    await_bytes(row_part.at[pl.ds(0, 31)], sent_sem.at[2])
    await_rows(1472, sent_sem.at[3])


def on_device(molecules, texts):
    dma = pltpu.SemaphoreType.DMA
    both = pl.pallas_call(
        kernel,
        out_shape=jax.ShapeDtypeStruct((2, SHARD, D), F32),
        in_specs=[pl.BlockSpec(memory_space=pl.ANY)] * 2,
        out_specs=pl.BlockSpec(memory_space=pltpu.VMEM),
        scratch_shapes=[
            pltpu.VMEM((MOLS, D), BF16),
            pltpu.VMEM((TEXTS, D), BF16),
            pltpu.VMEM((MOLS, TEXTS), F32),
            pltpu.VMEM((MOLS, TEXTS), F32),
            pltpu.VMEM((MOLS, TEXTS), BF16),
            pltpu.VMEM((MOLS, 128), F32),
            pltpu.VMEM((8, 8, TEXTS), F32),
            pltpu.VMEM((8, 8, TEXTS), F32),
            pltpu.VMEM((32, 8, 128), F32),
            pltpu.VMEM((16, 8, 128), F32),
            pltpu.VMEM((MOLS, D), F32),
            pltpu.VMEM((MOLS, D), BF16),
            pltpu.VMEM((2, 2, 4, 4, HALF, D), BF16),
            pltpu.VMEM((2, 2, 4, HALF, D), BF16),
            pltpu.VMEM((2, 2, 4, HALF, D), BF16),
            pltpu.VMEM((2, HALF, D), BF16),
            pltpu.VMEM((2, HALF, D), BF16),
            pltpu.VMEM((TEXTS // 2, D), F32),
            pltpu.VMEM((TEXTS // 2, D), BF16),
            pltpu.VMEM((TEXTS // 2, D), BF16),
            pltpu.VMEM((7, SHARD, D), BF16),
            pltpu.VMEM((7, SHARD, D), BF16),
            dma((4,)),
            dma((1,)),
            dma((1,)),
            dma((2, 4)),
            dma((1,)),
            dma((5,)),
            dma((2,)),
            dma((1,)),
            dma((1,)),
            dma((1,)),
            dma((1,)),
            dma((3,)),
            dma((2, 4)),
            dma((2,)),
            dma((1,)),
        ],
        compiler_params=pltpu.CompilerParams(
            collective_id=0, has_side_effects=True, vmem_limit_bytes=60 << 20
        ),
    )(molecules, texts)
    return both[0], both[1]


def solution(mesh):
    spec = P(("blk", "grp"), None)
    return jax.shard_map(
        on_device, mesh=mesh, in_specs=(spec, spec), out_specs=(spec, spec), check_vma=False
    )
```

time: 68.1 us -> 57.8 us (0.85)
  Pallas kernels: 65 us -> 55.4 us
    pallas_call x1, Pallas kernels: 65 us -> 55.4 us  [on_device(): pl.pallas_call(kernel, out_shape=jax.ShapeDtypeStruct((2, SHARD, D), F32)...]
    unnamed x4 -> x0, local copies, waits for them, and re-layouts: 1.55 us -> none
    squeeze x1, local copies, waits for them, and re-layouts: 0.67 us -> 1.6 us  [on_device(): return (both[0], both[1])]
where the time goes in v2:
time: 57.8 us; the launch traced here: 57.6 us
  Pallas kernels  55.4 us (96%)
  local copies, waits for them, and re-layouts  1.6 us (3%)
  between operations  0.64 us (1%)
    pallas_call x1, Pallas kernels, on_device(): pl.pallas_call(kernel, out_shape=jax.ShapeDtypeStruct((2, SHARD, D), F32)...  55.4 us
    squeeze x1, local copies, waits for them, and re-layouts, on_device(): return (both[0], both[1])  1.6 us

profile of v2, /device:TPU:1, one launch (start us, length us, event | category | flops | bytes accessed | tf_op | source)
XLA Modules:
  0.0 57.6 jit_solution(13986951410647540674)
XLA Ops:
  0.6 55.4 %shard_map.41 = f32[2,32,640]{2,1,0:T(8,128)} custom-call(bf16[32,640]{1,0:T(8,128)(2,1)} %mol_in.1, bf16[32,640]{1,0:T(8,128)(2,1)} %text_in.1), custom_call_target="tpu_custom_call" | custom-call | tf_op jit(solution)/shard_map/pallas_call | solution.py:383
  56.0 1.6 %slice_bitcast_fusion = (f32[32,640]{1,0:T(8,128)}, f32[32,640]{1,0:T(8,128)}) fusion(f32[2,32,640]{2,1,0:T(8,128)} %shard_map.41), kind=kLoop, calls=%fused_computation | loop fusion | bytes 327680 | tf_op jit(solution)/shard_map/squeeze | solution.py:431

commit v3 on v2

--- a/solution.py
+++ b/solution.py
@@ -121,7 +121,7 @@
         starts = [mol_row(0, q_, plus(x, e, 4), y), mol_row(1, q_, x, plus(y, e, 4))]
         for d in (1, 3, 2):
             for h in (0, 1):
-                mol_send_rows(starts[h], HALF, mol2_sem.at[0], second_peer[h](d))
+                mol_send_rows(starts[h], HALF, mol2_sem.at[own], second_peer[h](d))
 
     def fan_arrived(own, e):
         await_rows(2 * HALF, mol1_sem.at[own, 4 - e])
@@ -129,40 +129,47 @@
     def to_sibling(d):
         text_send_rows(plus(p, d, 8), c, sib_sem.at[0], sibling)
 
+    def forward(i, source, d, part):
+        text_send_rows(plus(p, source, 8), c, far_sem.at[i], p_peer(d), *part)
+
+    for i, (d, part) in enumerate(((2, low), (-2, high))):
+        text_send_rows(p, c, near_sem.at[i], p_peer(d), *part)
     for h in (0, 1):
         mol_send_rows(own_row[h], HALF, pair_sem.at[0], partner)
-    for i, (d, part) in enumerate(((2, low), (-2, high), (2, high), (-2, low))):
-        text_send_rows(p, c, near_sem.at[i], p_peer(d), *part)
+    for i, (d, part) in enumerate(((2, high), (-2, low))):
+        text_send_rows(p, c, near_sem.at[i + 2], p_peer(d), *part)
     fan(1)
-    spread(1, 0)
-    for d in (1, -1):
-        text_send_rows(p, c, near_sem.at[4], p_peer(d))
     to_sibling(0)
     await_rows(2 * HALF, pair_sem.at[0])
+    spread(0, 0)
     fan(0)
-    spread(0, 0)
-    for e in (1, 3, 2):
-        fan_arrived(1, e)
-        spread(1, e)
-
-    def forward(i, source, d, part):
-        text_send_rows(plus(p, source, 8), c, far_sem.at[i], p_peer(d), *part)
-
+    fan_arrived(1, 2)
+    spread(1, 2)
     await_rows(HALF, near_sem.at[0])
     forward(0, -2, 2, low)
     forward(1, -2, 1, low)
+    fan_arrived(1, 1)
+    spread(1, 1)
+    fan_arrived(1, 3)
+    spread(1, 3)
     await_rows(HALF, near_sem.at[1])
     forward(0, 2, -2, high)
     forward(1, 2, -1, high)
-    for e in (1, 3, 2):
-        fan_arrived(0, e)
-        spread(0, e)
+    for d in (1, -1):
+        text_send_rows(p, c, near_sem.at[4], p_peer(d))
     await_rows(HALF, near_sem.at[2])
     forward(1, -2, 1, high)
     to_sibling(-2)
     await_rows(HALF, near_sem.at[3])
     forward(1, 2, -1, low)
     to_sibling(2)
+    spread(1, 0)
+    fan_arrived(0, 3)
+    spread(0, 3)
+    fan_arrived(0, 1)
+    spread(0, 1)
+    fan_arrived(0, 2)
+    spread(0, 2)
     await_rows(2 * SHARD, near_sem.at[4])
     to_sibling(-1)
     to_sibling(1)
@@ -171,26 +178,33 @@
     to_sibling(3)
     await_rows(SHARD, far_sem.at[0])
     to_sibling(4)
-    await_rows(48 * HALF, mol2_sem.at[0])
     await_rows(8 * SHARD, sib_sem.at[0])
-    await_rows(1472, sent_sem.at[0])
-
-    scores[...] = lax.dot_general(
-        mol[...], text[...], (((1,), (1,)), ((), ())), preferred_element_type=F32
-    ) * (INVERSE_TEMP * LOG2E)
+
     row_me = (x * 4 + y) * 2 + q
     col_me = c * 8 + p
     lanes = [slice(128 * k, 128 * k + 128) for k in range(TEXTS // 128)]
 
-    def column_totals(b, carry):
+    def column_totals(b):
         for lane in lanes:
             tiles = scores[pl.ds(pl.multiple_of(b * 128, 128), 128), lane].reshape(16, 8, 128)
             top = jnp.max(tiles, axis=0)
             col_top[b, :, lane] = top
             col_mass[b, :, lane] = jnp.sum(jnp.exp2(tiles - top[None]), axis=0)
-        return carry
-
-    lax.fori_loop(0, MOLS // 128, column_totals, 0)
+
+    def score(q_):
+        for h in (0, 1):
+            block = rows(mol_row(h, q_, 0, 0), MOLS // 4)
+            scores[block, :] = lax.dot_general(
+                mol[block, :], text[...], (((1,), (1,)), ((), ())), preferred_element_type=F32
+            ) * (INVERSE_TEMP * LOG2E)
+            for i in (0, 1):
+                column_totals(h * 4 + q_ * 2 + i)
+
+    await_rows(24 * HALF, mol2_sem.at[1])
+    score(q)
+    await_rows(24 * HALF, mol2_sem.at[0])
+    score(other_q)
+    await_rows(1472, sent_sem.at[0])
     for k, lane in enumerate(lanes):
         top = col_top[:, :, lane].reshape(64, 128)
         overall = jnp.max(top, axis=0, keepdims=True)
@@ -264,10 +278,6 @@
     def text_part(c_):
         lane = pl.ds(pl.multiple_of(c_ * (TEXTS // 2), TEXTS // 2), TEXTS // 2)
         return lax.dot_general(weights[:, lane], mol[...], (((0,), (0,)), ((), ())), preferred_element_type=F32)
-
-    text_send[...] = text_part(1 - c).astype(BF16)
-    send(text_send, text_recv0, 3, rs_sib_sem.at[0], sibling)
-    text_sum[...] = text_part(c)
 
     def mol_parts(own):
         for h in (0, 1):
@@ -291,31 +301,12 @@
                         second_peer[h](d),
                     )
 
-    mol_parts(0)
-
-    await_rows(TEXTS // 2, rs_sib_sem.at[0])
-    text_sum[...] = text_sum[...] + text_recv0[...].astype(F32)
-
     def text_block(d, part=(0, SHARD)):
         return text_sum[pl.ds(pl.multiple_of(plus(p, d, 8) * SHARD + part[0], HALF), part[1]), :]
-
-    for slot, d in enumerate((4, 3, -3, 1, -1)):
-        text_send1[slot] = text_block(d).astype(BF16)
 
     def text_pass(i, slot, part, d):
         span = pl.ds(part[0], part[1])
         send(text_send1.at[slot, span], text_recv1.at[slot, span], 3, rs_text_sem.at[i], p_peer(d))
-
-    text_pass(1, 0, low, 2)
-    text_pass(1, 0, high, -2)
-    text_pass(0, 1, high, 1)
-    text_pass(0, 2, low, -1)
-    text_pass(1, 1, low, 1)
-    text_pass(1, 2, high, -1)
-    text_pass(2, 3, (0, SHARD), 1)
-    text_pass(2, 4, (0, SHARD), -1)
-
-    mol_parts(1)
 
     def text_pass2(d, part, *arrived):
         total = text_block(d, part)
@@ -345,10 +336,28 @@
             block = block + mol_recv2[h, own, d].astype(F32)
         return block
 
+    text_send[...] = text_part(1 - c).astype(BF16)
+    send(text_send, text_recv0, 3, rs_sib_sem.at[0], sibling)
+    mol_parts(0)
+    text_sum[...] = text_part(c)
+    await_rows(TEXTS // 2, rs_sib_sem.at[0])
+    text_sum[...] = text_sum[...] + text_recv0[...].astype(F32)
+    for slot, d in enumerate((4, 3, -3, 1, -1)):
+        text_send1[slot] = text_block(d).astype(BF16)
+
+    text_pass(0, 1, high, 1)
+    text_pass(0, 2, low, -1)
+    text_pass(1, 0, low, 2)
+    text_pass(1, 0, high, -2)
+    text_pass(1, 1, low, 1)
+    text_pass(1, 2, high, -1)
+    mol_parts(1)
     mol_pass2(0, 2)
     await_rows(SHARD, rs_text_sem.at[0])
     text_pass2(2, high, 1)
     text_pass2(-2, low, 2)
+    text_pass(2, 3, (0, SHARD), 1)
+    text_pass(2, 4, (0, SHARD), -1)
     mol_pass2(0, 1)
     mol_pass2(0, 3)
     await_rows(2 * SHARD, rs_text_sem.at[1])
@@ -412,7 +421,7 @@
             dma((1,)),
             dma((1,)),
             dma((2, 4)),
-            dma((1,)),
+            dma((2,)),
             dma((5,)),
             dma((2,)),
             dma((1,)),

time: 57.8 us -> 56 us (0.969)
  Pallas kernels: 55.4 us -> 53.2 us
    pallas_call x1, Pallas kernels: 55.4 us -> 53.2 us  [on_device(): pl.pallas_call(kernel, out_shape=jax.ShapeDtypeStruct((2, SHARD, D), F32)...]
where the time goes in v3:
time: 56 us; the launch traced here: 55.4 us
  Pallas kernels  53.2 us (95%)
  local copies, waits for them, and re-layouts  1.6 us (3%)
  between operations  0.64 us (1%)
    pallas_call x1, Pallas kernels, on_device(): pl.pallas_call(kernel, out_shape=jax.ShapeDtypeStruct((2, SHARD, D), F32)...  53.2 us
    squeeze x1, local copies, waits for them, and re-layouts, on_device(): return (both[0], both[1])  1.6 us

profile of v3, /device:TPU:1, one launch (start us, length us, event | category | flops | bytes accessed | tf_op | source)
XLA Modules:
  0.0 55.4 jit_solution(10548641776548328977)
XLA Ops:
  0.6 53.2 %shard_map.41 = f32[2,32,640]{2,1,0:T(8,128)} custom-call(bf16[32,640]{1,0:T(8,128)(2,1)} %mol_in.1, bf16[32,640]{1,0:T(8,128)(2,1)} %text_in.1), custom_call_target="tpu_custom_call" | custom-call | tf_op jit(solution)/shard_map/pallas_call | solution.py:392
  53.8 1.6 %slice_bitcast_fusion = (f32[32,640]{1,0:T(8,128)}, f32[32,640]{1,0:T(8,128)}) fusion(f32[2,32,640]{2,1,0:T(8,128)} %shard_map.41), kind=kLoop, calls=%fused_computation | loop fusion | bytes 327680 | tf_op jit(solution)/shard_map/squeeze | solution.py:440

commit v4 on v3

--- a/solution.py
+++ b/solution.py
@@ -141,13 +141,8 @@
     fan(1)
     to_sibling(0)
     await_rows(2 * HALF, pair_sem.at[0])
+    fan(0)
     spread(0, 0)
-    fan(0)
-    fan_arrived(1, 2)
-    spread(1, 2)
-    await_rows(HALF, near_sem.at[0])
-    forward(0, -2, 2, low)
-    forward(1, -2, 1, low)
     fan_arrived(1, 1)
     spread(1, 1)
     fan_arrived(1, 3)
@@ -155,6 +150,11 @@
     await_rows(HALF, near_sem.at[1])
     forward(0, 2, -2, high)
     forward(1, 2, -1, high)
+    await_rows(HALF, near_sem.at[0])
+    forward(0, -2, 2, low)
+    forward(1, -2, 1, low)
+    fan_arrived(1, 2)
+    spread(1, 2)
     for d in (1, -1):
         text_send_rows(p, c, near_sem.at[4], p_peer(d))
     await_rows(HALF, near_sem.at[2])
@@ -164,10 +164,10 @@
     forward(1, 2, -1, low)
     to_sibling(2)
     spread(1, 0)
+    fan_arrived(0, 1)
+    spread(0, 1)
     fan_arrived(0, 3)
     spread(0, 3)
-    fan_arrived(0, 1)
-    spread(0, 1)
     fan_arrived(0, 2)
     spread(0, 2)
     await_rows(2 * SHARD, near_sem.at[4])
@@ -229,13 +229,18 @@
         return carry
 
     lax.fori_loop(0, MOLS // 128, row_totals, 0)
-    for dx in (2, 1, 3, 0):
-        for dy in (2, 1, 3, 0):
-            for e in (0, 1):
-                if dx or dy or e:
+    for x_ in range(4):
+        for y_ in range(4):
+            for e in (1, 0):
+                def send_row():
                     block = row_part.at[row_me]
-                    target = device(plus(x, dx, 4), plus(y, dy, 4), p, q if e == 0 else other_q, c)
+                    target = device(x_, y_, p, q if e == 0 else other_q, c)
                     send(block, block, 2, row_sem.at[0], target)
+
+                if e:
+                    send_row()
+                else:
+                    pl.when(jnp.logical_or(x != x_, y != y_))(send_row)
 
     def merge(parts):
         top = jnp.max(parts, axis=0)
@@ -302,7 +307,8 @@
                     )
 
     def text_block(d, part=(0, SHARD)):
-        return text_sum[pl.ds(pl.multiple_of(plus(p, d, 8) * SHARD + part[0], HALF), part[1]), :]
+        block = rows(plus(p, d, 8) * SHARD + part[0], part[1])
+        return text_sum[block, :] + text_recv0[block, :].astype(F32)
 
     def text_pass(i, slot, part, d):
         span = pl.ds(part[0], part[1])
@@ -341,16 +347,20 @@
     mol_parts(0)
     text_sum[...] = text_part(c)
     await_rows(TEXTS // 2, rs_sib_sem.at[0])
-    text_sum[...] = text_sum[...] + text_recv0[...].astype(F32)
-    for slot, d in enumerate((4, 3, -3, 1, -1)):
+    def text_ready(slot, d):
         text_send1[slot] = text_block(d).astype(BF16)
 
+    text_ready(1, 3)
     text_pass(0, 1, high, 1)
+    text_ready(2, -3)
     text_pass(0, 2, low, -1)
+    text_ready(0, 4)
     text_pass(1, 0, low, 2)
     text_pass(1, 0, high, -2)
     text_pass(1, 1, low, 1)
     text_pass(1, 2, high, -1)
+    text_ready(3, 1)
+    text_ready(4, -1)
     mol_parts(1)
     mol_pass2(0, 2)
     await_rows(SHARD, rs_text_sem.at[0])

time: 56 us -> 55.2 us (0.986)
  no operation moved by 1% of the time
where the time goes in v4:
time: 55.2 us; the launch traced here: 55 us
  Pallas kernels  52.8 us (96%)
  local copies, waits for them, and re-layouts  1.6 us (3%)
  between operations  0.64 us (1%)
    pallas_call x1, Pallas kernels, on_device(): pl.pallas_call(kernel, out_shape=jax.ShapeDtypeStruct((2, SHARD, D), F32)...  52.8 us
    squeeze x1, local copies, waits for them, and re-layouts, on_device(): return (both[0], both[1])  1.6 us

profile of v4, /device:TPU:1, one launch (start us, length us, event | category | flops | bytes accessed | tf_op | source)
XLA Modules:
  0.0 55.0 jit_solution(12626508031653973837)
XLA Ops:
  0.6 52.8 %shard_map.41 = f32[2,32,640]{2,1,0:T(8,128)} custom-call(bf16[32,640]{1,0:T(8,128)(2,1)} %mol_in.1, bf16[32,640]{1,0:T(8,128)(2,1)} %text_in.1), custom_call_target="tpu_custom_call" | custom-call | tf_op jit(solution)/shard_map/pallas_call | solution.py:402
  53.4 1.6 %slice_bitcast_fusion = (f32[32,640]{1,0:T(8,128)}, f32[32,640]{1,0:T(8,128)}) fusion(f32[2,32,640]{2,1,0:T(8,128)} %shard_map.41), kind=kLoop, calls=%fused_computation | loop fusion | bytes 327680 | tf_op jit(solution)/shard_map/squeeze | solution.py:450

commit v5 on v4

--- a/solution.py
+++ b/solution.py
@@ -90,8 +90,8 @@
     for load in loads:
         load.start()
 
-    peers = [p_peer(d) for d in (1, -1, 2, -2)] + [partner, sibling]
-    peers += [x_peer(d) for d in (1, 2, 3)] + [y_peer(d) for d in (1, 2, 3)]
+    peers = [p_peer(d) for d in (2, -2, 1, -1)] + [x_peer(d) for d in (2, 1, 3)]
+    peers += [y_peer(d) for d in (2, 1, 3)] + [partner, sibling]
     barrier = pltpu.get_barrier_semaphore()
     for peer in peers:
         pl.semaphore_signal(barrier, inc=1, device_id=peer, device_id_type=MESH)

time: 55.2 us -> 55.2 us (level)
  no operation moved by 1% of the time
where the time goes in v5:
time: 55.2 us; the launch traced here: 55 us
  Pallas kernels  52.7 us (95%)
  local copies, waits for them, and re-layouts  1.6 us (3%)
  between operations  0.64 us (1%)
    pallas_call x1, Pallas kernels, on_device(): pl.pallas_call(kernel, out_shape=jax.ShapeDtypeStruct((2, SHARD, D), F32)...  52.7 us
    squeeze x1, local copies, waits for them, and re-layouts, on_device(): return (both[0], both[1])  1.6 us

profile of v5, /device:TPU:1, one launch (start us, length us, event | category | flops | bytes accessed | tf_op | source)
XLA Modules:
  0.0 55.0 jit_solution(5549210948376140111)
XLA Ops:
  0.6 52.7 %shard_map.41 = f32[2,32,640]{2,1,0:T(8,128)} custom-call(bf16[32,640]{1,0:T(8,128)(2,1)} %mol_in.1, bf16[32,640]{1,0:T(8,128)(2,1)} %text_in.1), custom_call_target="tpu_custom_call" | custom-call | tf_op jit(solution)/shard_map/pallas_call | solution.py:402
  53.4 1.6 %slice_bitcast_fusion = (f32[32,640]{1,0:T(8,128)}, f32[32,640]{1,0:T(8,128)}) fusion(f32[2,32,640]{2,1,0:T(8,128)} %shard_map.41), kind=kLoop, calls=%fused_computation | loop fusion | bytes 327680 | tf_op jit(solution)/shard_map/squeeze | solution.py:450
